TPU v7x, 32 devices: a whole 2x2x4 slice. The times are simulated.
32 devices in a mesh: path: 16 (over z, y, x), mod: 2 (over core).
Axes of the slice: x: 2, y: 2, z: 4, core: 2. Of those that a mesh axis runs over, the one named last changes fastest.
Arguments:
- tokens: bfloat16 [16, 384, 3072], P('path', None, 'mod'), may hold values from -48 to 48
- cotangent: bfloat16 [16, 384, 3072], P('path', None, 'mod'), may hold values from -1.5 to 1.5
- path_modules: int32 [16, 1], replicated, may hold values from 0 to 7, as said below
- path_in: bfloat16 [16, 1, 3072, 1024], P('path', None, 'mod'), may hold values from -0.109375 to 0.109375
- path_out: bfloat16 [16, 1, 3072, 1024], P('path', None, 'mod'), may hold values from -0.1875 to 0.1875
- outer_in: float32 [1, 8, 3072, 1024], P(None, None, ('mod', 'path')), may hold values from -0.109375 to 0.109375
- outer_out: float32 [1, 8, 3072, 1024], P(None, None, ('mod', 'path')), may hold values from -0.1875 to 0.1875
- moment_in: float32 [1, 8, 3072, 1024], P(None, None, ('mod', 'path')), may hold values from -0.125 to 0.125
- moment_out: float32 [1, 8, 3072, 1024], P(None, None, ('mod', 'path')), may hold values from -0.4375 to 0.4375
Outputs:
- block_out: bfloat16 [16, 384, 3072], P('path', None, 'mod')
- grad_in: bfloat16 [16, 1, 3072, 1024], P('path', None, 'mod')
- grad_out: bfloat16 [16, 1, 3072, 1024], P('path', None, 'mod')
Inputs may be any that keep to these rules, and one draw needn't show every extreme that they name: `path_modules`: every module of each level is read by at least one path.
All inputs are finite; a program needn't handle non-finite values.
Results may differ from a plain program's by a relative error of at most 0.0071.
Values may be sent and summed in bfloat16 or wider, within the bound.
A program may use at most 128 MiB of HBM per device.

v0:
```python
import jax
import jax.numpy as jnp
from jax import lax
from jax.sharding import PartitionSpec as P

D = 3072


epsilon = 1e-05
outer_rate = 0.7
outer_momentum = 0.9


def outer_step(outer, moment, average):
    delta = outer - average
    moment_next = outer_momentum * moment + delta
    return (outer - outer_rate * (delta + outer_momentum * moment_next)).astype(jnp.bfloat16)


def silu_slope(pre):
    sigmoid_z = jax.nn.sigmoid(pre)
    return sigmoid_z * (1.0 + pre * (1.0 - sigmoid_z))


def token_total(values):
    return lax.psum(values, "mod")


def share_total(left, right):
    return lax.psum_scatter(
        jnp.dot(left, right, preferred_element_type=jnp.float32),
        "mod",
        scatter_dimension=0,
        tiled=True,
    )


def share_gather(values):
    return lax.all_gather(values, "mod", axis=0, tiled=True)


def hidden_forward(normed, weight_level):
    pre_share = share_total(normed, weight_level)
    act_share = jax.nn.silu(pre_share).astype(jnp.bfloat16)
    return (pre_share, share_gather(act_share))


def hidden_backward(upstream, weight_level, pre):
    slope_share = share_total(upstream, weight_level)
    return share_gather((slope_share * silu_slope(pre)).astype(jnp.bfloat16))


def local(
    tokens, cotangent, path_modules, path_in, path_out, outer_in, outer_out, moment_in, moment_out
):
    path_count = lax.axis_size("path")
    level_count = path_in.shape[1]
    local_rows = path_in.shape[2]
    hidden = path_in.shape[3]
    module_count = outer_in.shape[1]
    owner_rows = outer_in.shape[2]
    piece_shape = (level_count, path_count, owner_rows, hidden)
    arrived_in, arrived_out = (
        lax.all_to_all(
            path_in.reshape(piece_shape), "path", split_axis=1, concat_axis=1, tiled=True
        ),
        lax.all_to_all(
            path_out.reshape(piece_shape), "path", split_axis=1, concat_axis=1, tiled=True
        ),
    )
    level = 0
    chosen = path_modules[:, level]
    member = chosen[None, :] == jnp.arange(module_count, dtype=jnp.int32)[:, None]
    counts = jnp.sum(member.astype(jnp.float32), axis=1)[:, None, None]
    member_bf = member.astype(jnp.bfloat16)
    summed_in = jnp.dot(
        member_bf,
        arrived_in[level].reshape(path_count, owner_rows * hidden),
        preferred_element_type=jnp.float32,
    )
    summed_out = jnp.dot(
        member_bf,
        arrived_out[level].reshape(path_count, owner_rows * hidden),
        preferred_element_type=jnp.float32,
    )
    fresh_in = outer_step(
        outer_in[level],
        moment_in[level],
        summed_in.reshape(module_count, owner_rows, hidden) / counts,
    )
    fresh_out = outer_step(
        outer_out[level],
        moment_out[level],
        summed_out.reshape(module_count, owner_rows, hidden) / counts,
    )
    picked_in = jnp.stack([jnp.take(fresh_in, path_modules[:, 0], axis=0)])
    picked_out = jnp.stack([jnp.take(fresh_out, path_modules[:, 0], axis=0)])
    back_in, back_out = (
        lax.all_to_all(picked_in, "path", split_axis=1, concat_axis=1, tiled=True),
        lax.all_to_all(picked_out, "path", split_axis=1, concat_axis=1, tiled=True),
    )
    weight_in = back_in.reshape(level_count, local_rows, hidden)
    weight_out = back_out.reshape(level_count, local_rows, hidden)
    state = tokens[0]
    level = 0
    wide = state.astype(jnp.float32)
    scale = lax.rsqrt(token_total(jnp.sum(wide * wide, axis=1)) / D + epsilon)[:, None]
    normal = wide * scale
    normed = normal.astype(jnp.bfloat16)
    pre, act = hidden_forward(normed, weight_in[level])
    branch = lax.dot_general(
        act, weight_out[level], (((1,), (1,)), ((), ())), preferred_element_type=jnp.float32
    )
    saved = [(scale, normal, normed, pre, act)]
    state = (wide + branch).astype(jnp.bfloat16)
    upstream = cotangent[0]
    grads_in = [None] * level_count
    grads_out = [None] * level_count
    for level in reversed(range(level_count)):
        scale, normal, normed, pre, act = saved[level]
        grads_out[level] = lax.dot_general(
            upstream, act, (((0,), (0,)), ((), ())), preferred_element_type=jnp.float32
        ).astype(jnp.bfloat16)
        pregrad = hidden_backward(upstream, weight_out[level], pre)
        grads_in[level] = lax.dot_general(
            normed, pregrad, (((0,), (0,)), ((), ())), preferred_element_type=jnp.float32
        ).astype(jnp.bfloat16)
    return (state[None], jnp.stack(grads_in)[None], jnp.stack(grads_out)[None])


def solution(mesh):
    return jax.shard_map(
        local,
        mesh=mesh,
        in_specs=(
            P("path", None, "mod"),
            P("path", None, "mod"),
            P(),
            P("path", None, "mod", None),
            P("path", None, "mod", None),
            P(None, None, ("mod", "path"), None),
            P(None, None, ("mod", "path"), None),
            P(None, None, ("mod", "path"), None),
            P(None, None, ("mod", "path"), None),
        ),
        out_specs=(
            P("path", None, "mod"),
            P("path", None, "mod", None),
            P("path", None, "mod", None),
        ),
        check_vma=False,
    )
```

profile of v0, /device:TPU:15, one launch (start us, length us, event | category | flops | bytes accessed | tf_op | source)
XLA Modules:
  0.0 375.9 jit_solution(5742707561376320261)
XLA Ops:
  7.2 75.5 %all_to_all.20 = bf16[1,16,96,1024]{3,2,0,1:T(8,128)(2,1)} all-to-all(bf16[1,16,96,1024]{3,2,0,1:T(8,128)(2,1)} %bitcast.125), channel_id=1, replica_groups=mesh['path'=16,'mod'=2] {'path'}, dimensions={1} | all-to-all | bytes 6291456 | tf_op jit(solution)/shard_map/all_to_all | solution.py:64
  82.7 5.9 %all-to-all-start.2 = ((bf16[1,16,96,1024]{3,2,0,1:T(8,128)(2,1)}), bf16[1,16,96,1024]{3,2,0,1:T(8,128)(2,1)}, u32[]{:S(2)}, u32[]{:S(2)}) async-start(bf16[1,16,96,1024]{3,2,0,1:T(8,128)(2,1)} %bitcast.126), calls=%async_computation.3 | async-start | bytes 6291456 | tf_op jit(solution)/shard_map/all_to_all | solution.py:67
  88.7 10.5 %fusion.17 = bf16[8,96,1024]{2,0,1:T(8,128)(2,1)S(1)} fusion(f32[1,8,96,1024]{3,2,1,0:T(8,128)} %param.18, f32[1,8,96,1024]{3,2,1,0:T(8,128)} %param.16, f32[8]{0:T(128)S(1)} %convert_reduce_fusion, s32[16]{0:T(128)S(1)} %bitcast.130, bf16[2,8,96,1024]{3,2,1,0:T(8,128)(2,1)} %bitcast.128), kind=kOutput, calls=%fused_computation.24 | convolution fusion | flops 32243840 | bytes 11010144 | tf_op jit(solution)/shard_map/dot_general | solution.py:76
  99.2 0.9 copy.29
  100.1 58.7 %all-to-all-done.2 = bf16[1,16,96,1024]{3,2,0,1:T(8,128)(2,1)} async-done(((bf16[1,16,96,1024]{3,2,0,1:T(8,128)(2,1)}), bf16[1,16,96,1024]{3,2,0,1:T(8,128)(2,1)}, u32[]{:S(2)}, u32[]{:S(2)}) %all-to-all-start.2) | async-done | bytes 3145760 | tf_op jit(solution)/shard_map/all_to_all | solution.py:67
  158.8 10.7 %fusion.12 = bf16[8,96,1024]{2,0,1:T(8,128)(2,1)S(1)} fusion(f32[1,8,96,1024]{3,2,1,0:T(8,128)} %param.19, f32[1,8,96,1024]{3,2,1,0:T(8,128)} %param.17, f32[8]{0:T(128)S(1)} %convert_reduce_fusion, s32[16]{0:T(128)S(1)} %bitcast.131, bf16[2,8,96,1024]{3,2,1,0:T(8,128)(2,1)} %bitcast.37), kind=kOutput, calls=%fused_computation.17 | convolution fusion | flops 32243840 | bytes 11010144 | tf_op jit(solution)/shard_map/dot_general | solution.py:81
  169.5 2.0 copy.34
  171.5 2.4 gather_fusion
  173.9 3.8 %gather_fusion.1 = bf16[16,96,1024]{2,1,0:T(8,128)(2,1)} fusion(bf16[8,96,1024]{2,1,0:T(8,128)(2,1)} %copy.34, s32[1024]{0:T(1024)S(1)} %pad_clamp_fusion), kind=kCustom, calls=%fused_computation.1.clone | custom fusion | bytes 6291520 | tf_op jit(solution)/shard_map/jit(_take)/gather | solution.py:97
  177.7 5.1 %select_bitcast_fusion = (bf16[1,16,96,1024]{3,2,0,1:T(8,128)(2,1)}, bf16[1,16,96,1024]{3,2,0,1:T(8,128)(2,1)S(1)}) fusion(bf16[16,96,1024]{2,1,0:T(8,128)(2,1)} %gather_fusion.1, pred[16]{0:T(512)(128)(4,1)S(1)} %compare_and_fusion, bf16[16,96,1024]{2,1,0:T(8,128)(2,1)} %gather_fusion), kind=kLoop, calls=%fused_computation.28 | loop fusion | flops 3145728 | bytes 12582928 | tf_op jit(solution)/shard_map/stack | solution.py:97
  182.8 73.2 %all_to_all.21 = bf16[1,16,96,1024]{3,2,0,1:T(8,128)(2,1)} all-to-all(bf16[1,16,96,1024]{3,2,0,1:T(8,128)(2,1)S(1)} %get-tuple-element.16), channel_id=1, replica_groups=mesh['path'=16,'mod'=2] {'path'}, dimensions={1} | all-to-all | bytes 6291456 | tf_op jit(solution)/shard_map/all_to_all | solution.py:99
  256.1 6.0 %all-to-all-start.3 = ((bf16[1,16,96,1024]{3,2,0,1:T(8,128)(2,1)}), bf16[1,16,96,1024]{3,2,0,1:T(8,128)(2,1)}, u32[]{:S(2)}, u32[]{:S(2)}) async-start(bf16[1,16,96,1024]{3,2,0,1:T(8,128)(2,1)} %get-tuple-element.15), calls=%async_computation.4 | async-start | bytes 6291456 | tf_op jit(solution)/shard_map/all_to_all | solution.py:100
  262.4 4.6 %psum.7 = f32[384]{0:T(512)S(1)} all-reduce(f32[384]{0:T(512)S(1)} %fusion.22), channel_id=1, replica_groups=mesh['path'=16,'mod'=2] {'mod'}, use_global_device_ids=true, to_apply=%region_1.2 | all-reduce | flops 384 | bytes 3072 | tf_op jit(solution)/shard_map/psum | solution.py:26
  267.0 4.5 %fusion.30 = f32[384,1024]{1,0:T(8,128)} fusion(bf16[1536,1024]{1,0:T(8,128)(2,1)} %bitcast.127, bf16[1,384,1536]{2,1,0:T(8,128)(2,1)S(1)} %copy-done.1, f32[384]{0:T(512)S(1)} %add_rsqrt_fusion), kind=kOutput, calls=%fused_computation.42 | convolution fusion | flops 1209729024 | bytes 5899776 | tf_op jit(solution)/shard_map/dot_general | solution.py:31
  271.6 60.7 %all-to-all-done.3 = bf16[1,16,96,1024]{3,2,0,1:T(8,128)(2,1)} async-done(((bf16[1,16,96,1024]{3,2,0,1:T(8,128)(2,1)}), bf16[1,16,96,1024]{3,2,0,1:T(8,128)(2,1)}, u32[]{:S(2)}, u32[]{:S(2)}) %all-to-all-start.3) | async-done | bytes 3145760 | tf_op jit(solution)/shard_map/all_to_all | solution.py:100
  332.2 4.4 %convolution_bitcast_fusion = f32[384,1024]{1,0:T(8,128)} fusion(bf16[1536,1024]{1,0:T(8,128)(2,1)} %bitcast.17, bf16[1,384,1536]{2,1,0:T(8,128)(2,1)S(1)} %copy-done), kind=kOutput, calls=%fused_computation.40 | convolution fusion | flops 1207959552 | bytes 5898240 | tf_op jit(solution)/shard_map/dot_general | solution.py:31
  336.7 9.8 %reduce-scatter.5.cloned.1.call-done = f32[192,1024]{1,0:T(8,128)} async-done(((f32[384,1024]{1,0:T(8,128)}), f32[192,1024]{1,0:T(8,128)}) %reduce-scatter.5.cloned.1.call-update) | async-done | bytes 786448 | tf_op jit(solution)/shard_map/reduce_scatter | solution.py:30
  346.5 1.7 multiply_convert_fusion
  348.2 2.4 all_gather.6
  350.5 4.4 %fusion.21 = bf16[1,384,1536]{2,1,0:T(8,128)(2,1)} fusion(bf16[384,1024]{1,0:T(8,128)(2,1)S(1)} %all_gather.6, bf16[1536,1024]{1,0:T(8,128)(2,1)} %bitcast.17, bf16[1,384,1536]{2,1,0:T(8,128)(2,1)S(1)} %copy-done.1), kind=kOutput, calls=%fused_computation.36 | convolution fusion | flops 1209729024 | bytes 6291456 | tf_op jit(solution)/shard_map/dot_general | solution.py:111
  354.9 3.5 fusion.1
  358.4 4.6 %copy.37 = bf16[1,1,1536,1024]{3,2,1,0:T(8,128)(2,1)} copy(bf16[1,1,1536,1024]{2,3,1,0:T(8,128)(2,1)} %fusion.1) | data formatting | bytes 6291456
  363.1 2.4 all_gather.7
  365.4 3.6 fusion
  (17 shorter events, 0.6 us)
Async XLA Ops:
  7.2 325.1 %copy-start = (bf16[1,384,1536]{2,1,0:T(8,128)(2,1)S(1)}, bf16[1,384,1536]{2,1,0:T(8,128)(2,1)}, u32[]{:S(2)}) copy-start(bf16[1,384,1536]{2,1,0:T(8,128)(2,1)} %param.12) | copy-start | bytes 3538948
  82.7 5.9 %copy-start.2 = (s32[16,1]{0,1:T(1,128)S(1)}, s32[16,1]{0,1:T(1,128)}, u32[]{:S(2)}) copy-start(s32[16,1]{0,1:T(1,128)} %param.13) | copy-start | bytes 196
  82.7 76.1 %all-to-all-start.2 = ((bf16[1,16,96,1024]{3,2,0,1:T(8,128)(2,1)}), bf16[1,16,96,1024]{3,2,0,1:T(8,128)(2,1)}, u32[]{:S(2)}, u32[]{:S(2)}) async-start(bf16[1,16,96,1024]{3,2,0,1:T(8,128)(2,1)} %bitcast.126), calls=%async_computation.3 | async-start | bytes 6291456 | tf_op jit(solution)/shard_map/all_to_all | solution.py:67
  256.1 6.0 %copy-start.1 = (bf16[1,384,1536]{2,1,0:T(8,128)(2,1)S(1)}, bf16[1,384,1536]{2,1,0:T(8,128)(2,1)}, u32[]{:S(2)}) copy-start(bf16[1,384,1536]{2,1,0:T(8,128)(2,1)} %param.11) | copy-start | bytes 3538948
  256.1 76.2 %all-to-all-start.3 = ((bf16[1,16,96,1024]{3,2,0,1:T(8,128)(2,1)}), bf16[1,16,96,1024]{3,2,0,1:T(8,128)(2,1)}, u32[]{:S(2)}, u32[]{:S(2)}) async-start(bf16[1,16,96,1024]{3,2,0,1:T(8,128)(2,1)} %get-tuple-element.15), calls=%async_computation.4 | async-start | bytes 6291456 | tf_op jit(solution)/shard_map/all_to_all | solution.py:100
  262.0 74.7 %reduce-scatter.3.cloned.1.call-start = ((), (), s32[]{:S(2)}) async-start(), calls=%async_computation.6 | async-start | bytes 2359296 | tf_op jit(solution)/shard_map/reduce_scatter | solution.py:30
  271.5 75.0 %reduce-scatter.5.cloned.1.call-start = ((), (), s32[]{:S(2)}) async-start(), calls=%async_computation.7 | async-start | bytes 2359296 | tf_op jit(solution)/shard_map/reduce_scatter | solution.py:30
Sparse Core Ops, SparseCore 0:
  271.6 10.3 reduce-scatter.2
  336.8 9.6 reduce-scatter.4
where the time goes:
time: 377 us; the launch traced here: 376 us
  blocking collectives  158 us (42%)
  waiting for transfers between devices  129 us (34%)
  matrix products  41.5 us (11%)
  between operations  14.1 us (4%)
  local copies, waits for them, and re-layouts  13.8 us (4%)
  starting transfers between devices  11.9 us (3%)
  other arithmetic  7.28 us (2%)
    all_to_all x1, blocking collectives, local(): lax.all_to_all(path_in.reshape(piece_shape), 'path', split_axis=1, concat...  75.5 us
    all_to_all x1, blocking collectives, local(): lax.all_to_all(picked_in, 'path', split_axis=1, concat_axis=1, tiled=True)  73.2 us
    all_to_all x1, waiting for transfers between devices, local(): lax.all_to_all(picked_out, 'path', split_axis=1, concat_axis=1, tiled=True)  60.7 us
    all_to_all x1, waiting for transfers between devices, local(): lax.all_to_all(path_out.reshape(piece_shape), 'path', split_axis=1, conca...  58.7 us
    dot_general x1, matrix products, local(): jnp.dot(member_bf, arrived_out[level].reshape(path_count, owner_rows * hi...  10.7 us
    dot_general x1, matrix products, local(): jnp.dot(member_bf, arrived_in[level].reshape(path_count, owner_rows * hid...  10.5 us
    reduce_scatter x2, waiting for transfers between devices, share_total(): lax.psum_scatter(jnp.dot(left, right, preferred_element_type=jnp.float32)...  9.79 us
    dot_general x2, matrix products, share_total(): jnp.dot(left, right, preferred_element_type=jnp.float32)  8.89 us
  transfers between devices with their start and end apart: 4, of which 3 were waited for; matrix products, arithmetic and copies ran while one was open for 6% of the time, Pallas kernels for 0%

commit v1 on v0

--- a/solution.py
+++ b/solution.py
@@ -1,6 +1,10 @@
+import functools
+
 import jax
 import jax.numpy as jnp
 from jax import lax
+from jax.experimental import pallas as pl
+from jax.experimental.pallas import tpu as pltpu
 from jax.sharding import PartitionSpec as P
 
 D = 3072
@@ -128,9 +132,376 @@
     return (state[None], jnp.stack(grads_in)[None], jnp.stack(grads_out)[None])
 
 
+MESH = pl.DeviceIdType.MESH
+F32 = jnp.float32
+BF16 = jnp.bfloat16
+TILE = 256
+
+
+def far_first(count):
+    return sorted(range(1, count), key=lambda step: (abs(2 * step - count), step))
+
+
+def fused_kernel(
+    dims,
+    pm_ref,
+    tok_hbm,
+    cot_hbm,
+    path_in,
+    path_out,
+    outer_in,
+    outer_out,
+    moment_in,
+    moment_out,
+    block_hbm,
+    gin_hbm,
+    gout_hbm,
+    arr_in,
+    arr_out,
+    outer_v,
+    moment_v,
+    fresh,
+    pick_in,
+    pick_out,
+    w_in,
+    w_out,
+    tok,
+    cot,
+    normed,
+    norm_mine,
+    norm_other,
+    pre_mine,
+    pre_other,
+    slope_mine,
+    slope_other,
+    act,
+    pregrad,
+    gin_v,
+    gout_v,
+    state_v,
+    member,
+    count,
+    send_sems,
+    recv_sems,
+    own_sems,
+    pair_send,
+    pair_recv,
+    load_sems,
+    out_sems,
+):
+    paths, modules, rows, owner, hidden, tokens, width = dims
+    me = lax.axis_index("path")
+    core = lax.axis_index("mod")
+    steps = far_first(paths)
+    tiles = hidden // TILE
+
+    barrier = pltpu.get_barrier_semaphore()
+    for step in steps:
+        pl.semaphore_signal(
+            barrier, inc=1, device_id=(lax.rem(me + step, paths), core), device_id_type=MESH
+        )
+    pl.semaphore_signal(barrier, inc=1, device_id=(me, 1 - core), device_id_type=MESH)
+    pl.semaphore_wait(barrier, paths)
+
+    def span(index):
+        return pl.ds(pl.multiple_of(index * owner, 16), owner)
+
+    def gather_copy(kind, step, whole, arrived):
+        dest = lax.rem(me + step, paths)
+        return pltpu.make_async_remote_copy(
+            src_ref=whole.at[span(dest)],
+            dst_ref=arrived.at[me],
+            send_sem=send_sems.at[kind, step],
+            recv_sem=recv_sems.at[kind, step],
+            device_id=(dest, core),
+            device_id_type=MESH,
+        )
+
+    def spread_copy(kind, step, picked, weight):
+        dest = lax.rem(me + step, paths)
+        return pltpu.make_async_remote_copy(
+            src_ref=picked.at[dest],
+            dst_ref=weight.at[span(me)],
+            send_sem=send_sems.at[kind, step],
+            recv_sem=recv_sems.at[kind, step],
+            device_id=(dest, core),
+            device_id_type=MESH,
+        )
+
+    def pair_copy(slot, source, target):
+        return pltpu.make_async_remote_copy(
+            src_ref=source,
+            dst_ref=target,
+            send_sem=pair_send.at[slot],
+            recv_sem=pair_recv.at[slot],
+            device_id=(me, 1 - core),
+            device_id_type=MESH,
+        )
+
+    for step in steps:
+        gather_copy(0, step, path_in, arr_in).start()
+    for step in steps:
+        gather_copy(1, step, path_out, arr_out).start()
+
+    own_in = pltpu.make_async_copy(path_in.at[span(me)], arr_in.at[me], own_sems.at[0])
+    own_out = pltpu.make_async_copy(path_out.at[span(me)], arr_out.at[me], own_sems.at[1])
+    load_tok = pltpu.make_async_copy(tok_hbm, tok, load_sems.at[0])
+    load_cot = pltpu.make_async_copy(cot_hbm, cot, load_sems.at[1])
+    load_outer = pltpu.make_async_copy(outer_in, outer_v, load_sems.at[2])
+    load_moment = pltpu.make_async_copy(moment_in, moment_v, load_sems.at[3])
+    for copy in (load_tok, load_cot, own_in, own_out, load_outer, load_moment):
+        copy.start()
+
+    for k in range(modules):
+        total = jnp.float32(0.0)
+        for p in range(paths):
+            flag = jnp.where(pm_ref[p, 0] == k, jnp.float32(1.0), jnp.float32(0.0))
+            member[k * paths + p] = flag
+            total = total + flag
+        count[k] = total
+
+    load_tok.wait()
+    block = 32
+
+    @pl.loop(0, tokens // block)
+    def _(i):
+        at = pl.ds(pl.multiple_of(i * block, block), block)
+        wide = tok[at, :].astype(F32)
+        norm_mine[at, :] = jnp.broadcast_to(
+            jnp.sum(wide * wide, axis=1, keepdims=True), (block, 128)
+        )
+
+    pair = pair_copy(0, norm_mine, norm_other)
+    pair.start()
+    pair.wait()
+
+    @pl.loop(0, tokens // block)
+    def _(i):
+        at = pl.ds(pl.multiple_of(i * block, block), block)
+        total = norm_mine[at, :][:, :1] + norm_other[at, :][:, :1]
+        scale = lax.rsqrt(total / width + epsilon)
+        normed[at, :] = (tok[at, :].astype(F32) * scale).astype(BF16)
+
+    load_cot.wait()
+
+    def update(arrived):
+        columns = hidden // TILE
+
+        @pl.loop(0, (owner // 16) * columns)
+        def _(i):
+            at = pl.ds(pl.multiple_of((i // columns) * 16, 16), 16)
+            col = pl.ds(pl.multiple_of((i % columns) * TILE, TILE), TILE)
+            sums = [jnp.zeros((16, TILE), F32) for _ in range(modules)]
+            for p in range(paths):
+                x = arrived[p, at, col].astype(F32)
+                for k in range(modules):
+                    sums[k] = sums[k] + member[k * paths + p] * x
+            for k in range(modules):
+                average = sums[k] / count[k]
+                fresh[k, at, col] = outer_step(
+                    outer_v[k, at, col], moment_v[k, at, col], average
+                )
+
+    def spread(kind, picked, weight):
+        for step in steps:
+            dest = lax.rem(me + step, paths)
+            picked[dest] = fresh[pm_ref[dest, 0]]
+            spread_copy(kind, step, picked, weight).start()
+        weight[span(me), :] = fresh[pm_ref[me, 0]]
+
+    own_in.wait()
+    load_outer.wait()
+    load_moment.wait()
+    for step in steps:
+        gather_copy(0, step, path_in, arr_in).wait_recv()
+    update(arr_in)
+    load_outer = pltpu.make_async_copy(outer_out, outer_v, load_sems.at[2])
+    load_moment = pltpu.make_async_copy(moment_out, moment_v, load_sems.at[3])
+    load_outer.start()
+    load_moment.start()
+    spread(2, pick_in, w_in)
+
+    own_out.wait()
+    load_outer.wait()
+    load_moment.wait()
+    for step in steps:
+        gather_copy(1, step, path_out, arr_out).wait_recv()
+    update(arr_out)
+    spread(3, pick_out, w_out)
+
+    for step in steps:
+        spread_copy(2, step, pick_in, w_in).wait_recv()
+
+    @pl.loop(0, tiles)
+    def _(j):
+        col = pl.ds(pl.multiple_of(j * TILE, TILE), TILE)
+        pre_mine[j] = jnp.dot(normed[...], w_in[:, col], preferred_element_type=F32)
+
+    pair = pair_copy(1, pre_mine, pre_other)
+    pair.start()
+    pair.wait()
+
+    for j in range(tiles):
+
+        @pl.loop(0, tokens // block)
+        def _(i):
+            at = pl.ds(pl.multiple_of(i * block, block), block)
+            pre = pre_mine[j, at, :] + pre_other[j, at, :]
+            sigmoid = jax.nn.sigmoid(pre)
+            act[at, j * TILE : (j + 1) * TILE] = (pre * sigmoid).astype(BF16)
+            pre_mine[j, at, :] = sigmoid * (1.0 + pre * (1.0 - sigmoid))
+
+    @pl.loop(0, tiles)
+    def _(j):
+        col = pl.ds(pl.multiple_of(j * TILE, TILE), TILE)
+        gout_v[:, col] = lax.dot_general(
+            cot[...], act[:, col], (((0,), (0,)), ((), ())), preferred_element_type=F32
+        ).astype(BF16)
+
+    store_gout = pltpu.make_async_copy(gout_v, gout_hbm, out_sems.at[0])
+    store_gout.start()
+
+    for step in steps:
+        spread_copy(3, step, pick_out, w_out).wait_recv()
+
+    pairs = []
+    for j in range(tiles):
+        slope_mine[j] = jnp.dot(
+            cot[...], w_out[:, j * TILE : (j + 1) * TILE], preferred_element_type=F32
+        )
+        pairs.append(pair_copy(2 + j, slope_mine.at[j], slope_other.at[j]))
+        pairs[-1].start()
+
+    @pl.loop(0, rows // TILE)
+    def _(j):
+        col = pl.ds(pl.multiple_of(j * TILE, TILE), TILE)
+        branch = lax.dot_general(
+            act[...], w_out[col, :], (((1,), (1,)), ((), ())), preferred_element_type=F32
+        )
+        state_v[:, col] = (tok[:, col].astype(F32) + branch).astype(BF16)
+
+    store_state = pltpu.make_async_copy(state_v, block_hbm, out_sems.at[1])
+    store_state.start()
+
+    stores = []
+    for j in range(tiles):
+        col = slice(j * TILE, (j + 1) * TILE)
+        pairs[j].wait()
+        pregrad[:, col] = ((slope_mine[j] + slope_other[j]) * pre_mine[j]).astype(BF16)
+        gin_v[:, col] = lax.dot_general(
+            normed[...], pregrad[:, col], (((0,), (0,)), ((), ())), preferred_element_type=F32
+        ).astype(BF16)
+        stores.append(
+            pltpu.make_async_copy(gin_v.at[:, col], gin_hbm.at[:, col], out_sems.at[2 + j])
+        )
+        stores[-1].start()
+
+    for step in steps:
+        gather_copy(0, step, path_in, arr_in).wait_send()
+        gather_copy(1, step, path_out, arr_out).wait_send()
+        spread_copy(2, step, pick_in, w_in).wait_send()
+        spread_copy(3, step, pick_out, w_out).wait_send()
+    store_gout.wait()
+    store_state.wait()
+    for store in stores:
+        store.wait()
+
+
+def fused(
+    tokens, cotangent, path_modules, path_in, path_out, outer_in, outer_out, moment_in, moment_out
+):
+    paths = lax.axis_size("path")
+    mods = lax.axis_size("mod")
+    rows, hidden = path_in.shape[2:]
+    modules, owner = outer_in.shape[1:3]
+    count = tokens.shape[1]
+    tiles = hidden // TILE
+    dims = (paths, modules, rows, owner, hidden, count, rows * mods)
+    any_space = pl.BlockSpec(memory_space=pl.ANY)
+    vmem = pltpu.VMEM
+    out = pl.pallas_call(
+        functools.partial(fused_kernel, dims),
+        out_shape=(
+            jax.ShapeDtypeStruct((count, rows), BF16),
+            jax.ShapeDtypeStruct((rows, hidden), BF16),
+            jax.ShapeDtypeStruct((rows, hidden), BF16),
+        ),
+        in_specs=[pl.BlockSpec(memory_space=pltpu.SMEM)] + [any_space] * 8,
+        out_specs=(any_space,) * 3,
+        scratch_shapes=[
+            vmem((paths, owner, hidden), BF16),
+            vmem((paths, owner, hidden), BF16),
+            vmem((modules, owner, hidden), F32),
+            vmem((modules, owner, hidden), F32),
+            vmem((modules, owner, hidden), BF16),
+            vmem((paths, owner, hidden), BF16),
+            vmem((paths, owner, hidden), BF16),
+            vmem((rows, hidden), BF16),
+            vmem((rows, hidden), BF16),
+            vmem((count, rows), BF16),
+            vmem((count, rows), BF16),
+            vmem((count, rows), BF16),
+            vmem((count, 128), F32),
+            vmem((count, 128), F32),
+            vmem((tiles, count, TILE), F32),
+            vmem((tiles, count, TILE), F32),
+            vmem((tiles, count, TILE), F32),
+            vmem((tiles, count, TILE), F32),
+            vmem((count, hidden), BF16),
+            vmem((count, hidden), BF16),
+            vmem((rows, hidden), BF16),
+            vmem((rows, hidden), BF16),
+            vmem((count, rows), BF16),
+            pltpu.SMEM((modules * paths,), F32),
+            pltpu.SMEM((modules,), F32),
+            pltpu.SemaphoreType.DMA((4, paths)),
+            pltpu.SemaphoreType.DMA((4, paths)),
+            pltpu.SemaphoreType.DMA((2,)),
+            pltpu.SemaphoreType.DMA((2 + tiles,)),
+            pltpu.SemaphoreType.DMA((2 + tiles,)),
+            pltpu.SemaphoreType.DMA((4,)),
+            pltpu.SemaphoreType.DMA((2 + tiles,)),
+        ],
+        compiler_params=pltpu.CompilerParams(
+            collective_id=0, has_side_effects=True, vmem_limit_bytes=62 * 1024 * 1024
+        ),
+        cost_estimate=pl.CostEstimate(
+            flops=10 * count * rows * hidden,
+            bytes_accessed=8 * rows * hidden * 2,
+            transcendentals=count * hidden,
+        ),
+    )(
+        path_modules,
+        tokens[0],
+        cotangent[0],
+        path_in[0, 0],
+        path_out[0, 0],
+        outer_in[0],
+        outer_out[0],
+        moment_in[0],
+        moment_out[0],
+    )
+    state, grad_in, grad_out = out
+    return (state[None], grad_in[None, None], grad_out[None, None])
+
+
+def device_program(*arrays):
+    level_count, rows, hidden = arrays[3].shape[1:]
+    owner = arrays[5].shape[2]
+    fits = (
+        level_count == 1
+        and lax.axis_size("mod") == 2
+        and owner % 16 == 0
+        and rows % TILE == 0
+        and hidden % TILE == 0
+        and arrays[0].shape[1] % 32 == 0
+    )
+    return fused(*arrays) if fits else local(*arrays)
+
+
 def solution(mesh):
     return jax.shard_map(
-        local,
+        device_program,
         mesh=mesh,
         in_specs=(
             P("path", None, "mod"),

time: 377 us -> 317 us (0.84)
  Pallas kernels: 0 us -> 307 us
  blocking collectives: 158 us -> 0 us
  waiting for transfers between devices: 129 us -> 0 us
  matrix products: 41.5 us -> 0 us
  between operations: 14.1 us -> 0.64 us
  starting transfers between devices: 11.9 us -> 0 us
  other arithmetic: 7.28 us -> 0 us
  local copies, waits for them, and re-layouts: 13.8 us -> 9.37 us
    pallas_call x0 -> x1, Pallas kernels: none -> 307 us  [fused(): pl.pallas_call(functools.partial(fused_kernel, dims), out_shape=(jax.Shap...]
    all_to_all x2 -> x0, blocking collectives: 149 us -> none  [the longest x1 75.5 us: local(): lax.all_to_all(path_in.reshape(piece_shape), 'path', split_axis=1, concat...]
    all_to_all x2 -> x0, waiting for transfers between devices: 119 us -> none  [the longest x1 60.7 us: local(): lax.all_to_all(picked_out, 'path', split_axis=1, concat_axis=1, tiled=True)]
    dot_general x7 -> x0, matrix products: 41.5 us -> none  [the longest x1 10.7 us: local(): jnp.dot(member_bf, arrived_out[level].reshape(path_count, owner_rows * hi...]
    all_to_all x2 -> x0, starting transfers between devices: 11.8 us -> none  [the longest x1 5.95 us: local(): lax.all_to_all(picked_out, 'path', split_axis=1, concat_axis=1, tiled=True)]
    reduce_scatter x2 -> x0, waiting for transfers between devices: 9.79 us -> none  [share_total(): lax.psum_scatter(jnp.dot(left, right, preferred_element_type=jnp.float32)...]
    gather x2 -> x0, local copies, waits for them, and re-layouts: 6.23 us -> none  [the longest x1 3.82 us: local(): picked_out = jnp.stack([jnp.take(fresh_out, path_modules[:, 0], axis=0)])]
    another operation x1 -> x0, other arithmetic: 5.13 us -> none  [local(): picked_out = jnp.stack([jnp.take(fresh_out, path_modules[:, 0], axis=0)])]
  transfers between devices with their start and end apart: 4 -> 0, of which waited for: 3 -> 0; matrix products, arithmetic and copies ran while one was open for 6% -> 0% of each run, Pallas kernels for 0% -> 0%
where the time goes in v1:
time: 317 us
  Pallas kernels  307 us (97%)
  local copies, waits for them, and re-layouts  9.37 us (3%)
    pallas_call x1, Pallas kernels, fused(): pl.pallas_call(functools.partial(fused_kernel, dims), out_shape=(jax.Shap...  307 us
    unnamed x6, local copies, waits for them, and re-layouts  9.37 us

profile of v1, /device:TPU:15, one launch (start us, length us, event | category | flops | bytes accessed | tf_op | source)
XLA Modules:
  0.0 316.8 jit_solution(17718477732784466811)
XLA Ops:
  0.6 1.3 copy.12.pm_ref
  2.0 306.8 %shard_map.112 = (bf16[384,1536]{1,0:T(8,128)(2,1)}, bf16[1536,1024]{1,0:T(8,128)(2,1)}, bf16[1536,1024]{1,0:T(8,128)(2,1)}) custom-call(s32[16,1]{1,0:T(8,128)} %copy.12.pm_ref, bf16[384,1536]{1,0:T(8,128)(2,1)} %bitcast.20, bf16[384,1536]{1,0:T(8,128)(2,1)} %bitcast.21, bf16[1536,1024]{1,0:T(8,128)(2,1)} %bitcast.14, bf16[1536,1024]{1,0:T(8,128)(2,1)} %bitcast.15, ...), custom_call_target="tpu_custom_call" | custom-call | flops 6039797760 | bytes 25165824 | tf_op jit(solution)/shard_map/pallas_call | solution.py:422
  308.8 2.4 copy.16
  311.1 0.0 copy-start
  311.1 4.0 %copy.17 = bf16[1,1,1536,1024]{3,2,1,0:T(8,128)(2,1)} copy(bf16[1,1,1536,1024]{3,2,1,0:T(8,128)(2,1)} %bitcast.12) | data formatting | bytes 6291456
  315.2 0.0 copy-done
  315.2 1.7 copy.18
Async XLA Ops:
  311.1 4.0 %copy-start = (bf16[1536,1024]{1,0:T(8,128)(2,1)S(1)}, bf16[1536,1024]{1,0:T(8,128)(2,1)}, u32[]{:S(2)}) copy-start(bf16[1536,1024]{1,0:T(8,128)(2,1)} %get-tuple-element.8) | copy-start | bytes 9437188

commit v2 on v1

--- a/solution.py
+++ b/solution.py
@@ -138,8 +138,24 @@
 TILE = 256
 
 
-def far_first(count):
-    return sorted(range(1, count), key=lambda step: (abs(2 * step - count), step))
+def step_order(count):
+    half = count // 2
+    far, near = list(range(half, count)), list(range(1, half))
+    order = []
+    while far or near:
+        order += far[:1] + near[:1]
+        far, near = far[1:], near[1:]
+    return order
+
+
+def partner(me, step, count):
+    if count & (count - 1):
+        return lax.rem(me + step, count)
+    other, bit = 0, 1
+    while bit < count:
+        other = other + bit * lax.rem(me // bit + (step // bit) % 2, 2)
+        bit *= 2
+    return other
 
 
 def fused_kernel(
@@ -192,13 +208,13 @@
     paths, modules, rows, owner, hidden, tokens, width = dims
     me = lax.axis_index("path")
     core = lax.axis_index("mod")
-    steps = far_first(paths)
+    steps = step_order(paths)
     tiles = hidden // TILE
 
     barrier = pltpu.get_barrier_semaphore()
     for step in steps:
         pl.semaphore_signal(
-            barrier, inc=1, device_id=(lax.rem(me + step, paths), core), device_id_type=MESH
+            barrier, inc=1, device_id=(partner(me, step, paths), core), device_id_type=MESH
         )
     pl.semaphore_signal(barrier, inc=1, device_id=(me, 1 - core), device_id_type=MESH)
     pl.semaphore_wait(barrier, paths)
@@ -207,7 +223,7 @@
         return pl.ds(pl.multiple_of(index * owner, 16), owner)
 
     def gather_copy(kind, step, whole, arrived):
-        dest = lax.rem(me + step, paths)
+        dest = partner(me, step, paths)
         return pltpu.make_async_remote_copy(
             src_ref=whole.at[span(dest)],
             dst_ref=arrived.at[me],
@@ -218,7 +234,7 @@
         )
 
     def spread_copy(kind, step, picked, weight):
-        dest = lax.rem(me + step, paths)
+        dest = partner(me, step, paths)
         return pltpu.make_async_remote_copy(
             src_ref=picked.at[dest],
             dst_ref=weight.at[span(me)],
@@ -304,7 +320,7 @@
 
     def spread(kind, picked, weight):
         for step in steps:
-            dest = lax.rem(me + step, paths)
+            dest = partner(me, step, paths)
             picked[dest] = fresh[pm_ref[dest, 0]]
             spread_copy(kind, step, picked, weight).start()
         weight[span(me), :] = fresh[pm_ref[me, 0]]

time: 317 us -> 305 us (0.962); the launches traced: 317 us -> 300 us
  Pallas kernels: 307 us -> 290 us
    pallas_call x1, Pallas kernels: 307 us -> 290 us  [fused(): pl.pallas_call(functools.partial(fused_kernel, dims), out_shape=(jax.Shap...]
where the time goes in v2:
time: 305 us; the launch traced here: 300 us
  Pallas kernels  290 us (95%)
  local copies, waits for them, and re-layouts  9.37 us (3%)
    pallas_call x1, Pallas kernels, fused(): pl.pallas_call(functools.partial(fused_kernel, dims), out_shape=(jax.Shap...  290 us
    unnamed x6, local copies, waits for them, and re-layouts  9.37 us

profile of v2, /device:TPU:15, one launch (start us, length us, event | category | flops | bytes accessed | tf_op | source)
XLA Modules:
  0.0 299.9 jit_solution(3693864557019701462)
XLA Ops:
  0.6 1.3 copy.12.pm_ref
  2.0 289.9 %shard_map.112 = (bf16[384,1536]{1,0:T(8,128)(2,1)}, bf16[1536,1024]{1,0:T(8,128)(2,1)}, bf16[1536,1024]{1,0:T(8,128)(2,1)}) custom-call(s32[16,1]{1,0:T(8,128)} %copy.12.pm_ref, bf16[384,1536]{1,0:T(8,128)(2,1)} %bitcast.20, bf16[384,1536]{1,0:T(8,128)(2,1)} %bitcast.21, bf16[1536,1024]{1,0:T(8,128)(2,1)} %bitcast.14, bf16[1536,1024]{1,0:T(8,128)(2,1)} %bitcast.15, ...), custom_call_target="tpu_custom_call" | custom-call | flops 6039797760 | bytes 25165824 | tf_op jit(solution)/shard_map/pallas_call | solution.py:438
  291.8 2.4 copy.16
  294.2 0.0 copy-start
  294.2 4.0 %copy.17 = bf16[1,1,1536,1024]{3,2,1,0:T(8,128)(2,1)} copy(bf16[1,1,1536,1024]{3,2,1,0:T(8,128)(2,1)} %bitcast.12) | data formatting | bytes 6291456
  298.2 0.0 copy-done
  298.2 1.7 copy.18
Async XLA Ops:
  294.2 4.0 %copy-start = (bf16[1536,1024]{1,0:T(8,128)(2,1)S(1)}, bf16[1536,1024]{1,0:T(8,128)(2,1)}, u32[]{:S(2)}) copy-start(bf16[1536,1024]{1,0:T(8,128)(2,1)} %get-tuple-element.8) | copy-start | bytes 9437188

commit v3 on v2

--- a/solution.py
+++ b/solution.py
@@ -170,8 +170,10 @@
     moment_in,
     moment_out,
     block_hbm,
-    gin_hbm,
-    gout_hbm,
+    act_hbm,
+    pregrad_hbm,
+    normed_t_hbm,
+    cot_t_hbm,
     arr_in,
     arr_out,
     outer_v,
@@ -189,11 +191,12 @@
     pre_mine,
     pre_other,
     slope_mine,
+    slope_sent,
     slope_other,
     act,
     pregrad,
-    gin_v,
-    gout_v,
+    normed_t,
+    cot_t,
     state_v,
     member,
     count,
@@ -300,6 +303,19 @@
 
     load_cot.wait()
 
+    @pl.loop(0, rows // TILE)
+    def _(j):
+        col = pl.ds(pl.multiple_of(j * TILE, TILE), TILE)
+        normed_t[col, :] = normed[:, col].astype(F32).T.astype(BF16)
+        cot_t[col, :] = cot[:, col].astype(F32).T.astype(BF16)
+
+    stores = [
+        pltpu.make_async_copy(normed_t, normed_t_hbm, out_sems.at[0]),
+        pltpu.make_async_copy(cot_t, cot_t_hbm, out_sems.at[1]),
+    ]
+    for store in stores:
+        store.start()
+
     def update(arrived):
         columns = hidden // TILE
 
@@ -367,15 +383,8 @@
             act[at, j * TILE : (j + 1) * TILE] = (pre * sigmoid).astype(BF16)
             pre_mine[j, at, :] = sigmoid * (1.0 + pre * (1.0 - sigmoid))
 
-    @pl.loop(0, tiles)
-    def _(j):
-        col = pl.ds(pl.multiple_of(j * TILE, TILE), TILE)
-        gout_v[:, col] = lax.dot_general(
-            cot[...], act[:, col], (((0,), (0,)), ((), ())), preferred_element_type=F32
-        ).astype(BF16)
-
-    store_gout = pltpu.make_async_copy(gout_v, gout_hbm, out_sems.at[0])
-    store_gout.start()
+    stores.append(pltpu.make_async_copy(act, act_hbm, out_sems.at[2]))
+    stores[-1].start()
 
     for step in steps:
         spread_copy(3, step, pick_out, w_out).wait_recv()
@@ -385,7 +394,8 @@
         slope_mine[j] = jnp.dot(
             cot[...], w_out[:, j * TILE : (j + 1) * TILE], preferred_element_type=F32
         )
-        pairs.append(pair_copy(2 + j, slope_mine.at[j], slope_other.at[j]))
+        slope_sent[j] = slope_mine[j].astype(BF16)
+        pairs.append(pair_copy(2 + j, slope_sent.at[j], slope_other.at[j]))
         pairs[-1].start()
 
     @pl.loop(0, rows // TILE)
@@ -396,31 +406,68 @@
         )
         state_v[:, col] = (tok[:, col].astype(F32) + branch).astype(BF16)
 
-    store_state = pltpu.make_async_copy(state_v, block_hbm, out_sems.at[1])
-    store_state.start()
-
-    stores = []
+    stores.append(pltpu.make_async_copy(state_v, block_hbm, out_sems.at[3]))
+    stores[-1].start()
+
     for j in range(tiles):
         col = slice(j * TILE, (j + 1) * TILE)
         pairs[j].wait()
-        pregrad[:, col] = ((slope_mine[j] + slope_other[j]) * pre_mine[j]).astype(BF16)
-        gin_v[:, col] = lax.dot_general(
-            normed[...], pregrad[:, col], (((0,), (0,)), ((), ())), preferred_element_type=F32
-        ).astype(BF16)
-        stores.append(
-            pltpu.make_async_copy(gin_v.at[:, col], gin_hbm.at[:, col], out_sems.at[2 + j])
-        )
-        stores[-1].start()
+        slope = slope_mine[j] + slope_other[j].astype(F32)
+        pregrad[:, col] = (slope * pre_mine[j]).astype(BF16)
+
+    stores.append(pltpu.make_async_copy(pregrad, pregrad_hbm, out_sems.at[4]))
+    stores[-1].start()
 
     for step in steps:
         gather_copy(0, step, path_in, arr_in).wait_send()
         gather_copy(1, step, path_out, arr_out).wait_send()
         spread_copy(2, step, pick_in, w_in).wait_send()
         spread_copy(3, step, pick_out, w_out).wait_send()
-    store_gout.wait()
-    store_state.wait()
     for store in stores:
         store.wait()
+
+
+def finish_kernel(state, act, pregrad, normed_t, cot_t, block_out, grad_in, grad_out):
+    block_out[...] = state[...]
+    grad_in[...] = jnp.dot(normed_t[...], pregrad[...], preferred_element_type=F32).astype(BF16)
+    grad_out[...] = jnp.dot(cot_t[...], act[...], preferred_element_type=F32).astype(BF16)
+
+
+def finish(state, act, pregrad, normed_t, cot_t):
+    count, rows = state.shape
+    hidden = act.shape[1]
+    steps = rows // TILE
+
+    def split(height, length):
+        return pl.BlockSpec((height, length), lambda i: (i, 0))
+
+    def whole(height, length):
+        return pl.BlockSpec((height, length), lambda i: (0, 0))
+
+    state_spec = pl.BlockSpec((count, TILE), lambda i: (0, i))
+    return pl.pallas_call(
+        finish_kernel,
+        grid=(steps,),
+        out_shape=(
+            jax.ShapeDtypeStruct((count, rows), BF16),
+            jax.ShapeDtypeStruct((rows, hidden), BF16),
+            jax.ShapeDtypeStruct((rows, hidden), BF16),
+        ),
+        in_specs=[
+            state_spec,
+            whole(count, hidden),
+            whole(count, hidden),
+            split(TILE, count),
+            split(TILE, count),
+        ],
+        out_specs=(state_spec, split(TILE, hidden), split(TILE, hidden)),
+        compiler_params=pltpu.CompilerParams(vmem_limit_bytes=62 * 1024 * 1024),
+        cost_estimate=pl.CostEstimate(
+            flops=4 * count * rows * hidden,
+            bytes_accessed=4 * rows * hidden + 8 * count * rows + 4 * count * hidden,
+            transcendentals=0,
+        ),
+    )(state, act, pregrad, normed_t, cot_t)
 
 
 def fused(
@@ -439,11 +486,13 @@
         functools.partial(fused_kernel, dims),
         out_shape=(
             jax.ShapeDtypeStruct((count, rows), BF16),
-            jax.ShapeDtypeStruct((rows, hidden), BF16),
-            jax.ShapeDtypeStruct((rows, hidden), BF16),
+            jax.ShapeDtypeStruct((count, hidden), BF16),
+            jax.ShapeDtypeStruct((count, hidden), BF16),
+            jax.ShapeDtypeStruct((rows, count), BF16),
+            jax.ShapeDtypeStruct((rows, count), BF16),
         ),
         in_specs=[pl.BlockSpec(memory_space=pltpu.SMEM)] + [any_space] * 8,
-        out_specs=(any_space,) * 3,
+        out_specs=(any_space,) * 5,
         scratch_shapes=[
             vmem((paths, owner, hidden), BF16),
             vmem((paths, owner, hidden), BF16),
@@ -462,11 +511,12 @@
             vmem((tiles, count, TILE), F32),
             vmem((tiles, count, TILE), F32),
             vmem((tiles, count, TILE), F32),
-            vmem((tiles, count, TILE), F32),
+            vmem((tiles, count, TILE), BF16),
+            vmem((tiles, count, TILE), BF16),
             vmem((count, hidden), BF16),
             vmem((count, hidden), BF16),
-            vmem((rows, hidden), BF16),
-            vmem((rows, hidden), BF16),
+            vmem((rows, count), BF16),
+            vmem((rows, count), BF16),
             vmem((count, rows), BF16),
             pltpu.SMEM((modules * paths,), F32),
             pltpu.SMEM((modules,), F32),
@@ -476,7 +526,7 @@
             pltpu.SemaphoreType.DMA((2 + tiles,)),
             pltpu.SemaphoreType.DMA((2 + tiles,)),
             pltpu.SemaphoreType.DMA((4,)),
-            pltpu.SemaphoreType.DMA((2 + tiles,)),
+            pltpu.SemaphoreType.DMA((5,)),
         ],
         compiler_params=pltpu.CompilerParams(
             collective_id=0, has_side_effects=True, vmem_limit_bytes=62 * 1024 * 1024
@@ -497,7 +547,7 @@
         moment_in[0],
         moment_out[0],
     )
-    state, grad_in, grad_out = out
+    state, grad_in, grad_out = finish(*out)
     return (state[None], grad_in[None, None], grad_out[None, None])
 
 

time: 305 us -> 302 us (level)
  local copies, waits for them, and re-layouts: 9.37 us -> 1.33 us
  Pallas kernels: 290 us -> 294 us
    pallas_call x0 -> x1, Pallas kernels: none -> 8.11 us  [finish(): pl.pallas_call(finish_kernel, grid=(steps,), out_shape=(jax.ShapeDtypeStr...]
    unnamed x6 -> x1, local copies, waits for them, and re-layouts: 9.37 us -> 1.33 us
    pallas_call x1, Pallas kernels: 290 us -> 286 us  [fused(): pl.pallas_call(functools.partial(fused_kernel, dims), out_shape=(jax.Shap...]
where the time goes in v3:
time: 302 us; the launch traced here: 296 us
  Pallas kernels  294 us (97%)
    pallas_call x1, Pallas kernels, fused(): pl.pallas_call(functools.partial(fused_kernel, dims), out_shape=(jax.Shap...  286 us
    pallas_call x1, Pallas kernels, finish(): pl.pallas_call(finish_kernel, grid=(steps,), out_shape=(jax.ShapeDtypeStr...  8.11 us

profile of v3, /device:TPU:15, one launch (start us, length us, event | category | flops | bytes accessed | tf_op | source)
XLA Modules:
  0.0 296.3 jit_solution(18155181909532208711)
XLA Ops:
  0.6 1.3 copy.12.pm_ref
  2.0 286.2 %shard_map.112 = (bf16[384,1536]{1,0:T(8,128)(2,1)}, bf16[384,1024]{1,0:T(8,128)(2,1)}, bf16[384,1024]{1,0:T(8,128)(2,1)}, bf16[1536,384]{1,0:T(8,128)(2,1)}, bf16[1536,384]{1,0:T(8,128)(2,1)}) custom-call(s32[16,1]{1,0:T(8,128)} %copy.12.pm_ref, bf16[384,1536]{1,0:T(8,128)(2,1)} %bitcast.17, bf16[384,1536]{1,0:T(8,128)(2,1)} %bitcast.18, ...), custom_call_target="tpu_custom_call" | custom-call | flops 6039797760 | bytes 25165824 | tf_op jit(solution)/shard_map/pallas_call | solution.py:485
  288.2 8.1 %shard_map.113 = (bf16[384,1536]{1,0:T(8,128)(2,1)}, bf16[1536,1024]{1,0:T(8,128)(2,1)}, bf16[1536,1024]{1,0:T(8,128)(2,1)}) custom-call(bf16[384,1536]{1,0:T(8,128)(2,1)} %get-tuple-element.11.state, bf16[384,1024]{1,0:T(8,128)(2,1)} %get-tuple-element.12.act, bf16[384,1024]{1,0:T(8,128)(2,1)} %get-tuple-element.13.pregrad, ...), custom_call_target="tpu_custom_call" | custom-call | flops 2415919104 | bytes 12582912 | tf_op jit(solution)/shard_map/pallas_call | solution.py:448

commit v4 on v3

--- a/solution.py
+++ b/solution.py
@@ -436,7 +436,8 @@
 def finish(state, act, pregrad, normed_t, cot_t):
     count, rows = state.shape
     hidden = act.shape[1]
-    steps = rows // TILE
+    steps = 2
+    tile = rows // steps
 
     def split(height, length):
         return pl.BlockSpec((height, length), lambda i: (i, 0))
@@ -444,7 +445,7 @@
     def whole(height, length):
         return pl.BlockSpec((height, length), lambda i: (0, 0))
 
-    state_spec = pl.BlockSpec((count, TILE), lambda i: (0, i))
+    state_spec = pl.BlockSpec((count, tile), lambda i: (0, i))
     return pl.pallas_call(
         finish_kernel,
         grid=(steps,),
@@ -457,10 +458,10 @@
             state_spec,
             whole(count, hidden),
             whole(count, hidden),
-            split(TILE, count),
-            split(TILE, count),
+            split(tile, count),
+            split(tile, count),
         ],
-        out_specs=(state_spec, split(TILE, hidden), split(TILE, hidden)),
+        out_specs=(state_spec, split(tile, hidden), split(tile, hidden)),
         compiler_params=pltpu.CompilerParams(vmem_limit_bytes=62 * 1024 * 1024),
         cost_estimate=pl.CostEstimate(
             flops=4 * count * rows * hidden,
@@ -558,7 +559,7 @@
         level_count == 1
         and lax.axis_size("mod") == 2
         and owner % 16 == 0
-        and rows % TILE == 0
+        and rows % (2 * TILE) == 0
         and hidden % TILE == 0
         and arrays[0].shape[1] % 32 == 0
     )

time: 302 us -> 300 us (level)
  no operation moved by 1% of the time
where the time goes in v4:
time: 300 us; the launch traced here: 295 us
  Pallas kernels  293 us (98%)
    pallas_call x1, Pallas kernels, fused(): pl.pallas_call(functools.partial(fused_kernel, dims), out_shape=(jax.Shap...  286 us
    pallas_call x1, Pallas kernels, finish(): pl.pallas_call(finish_kernel, grid=(steps,), out_shape=(jax.ShapeDtypeStr...  7.02 us

profile of v4, /device:TPU:15, one launch (start us, length us, event | category | flops | bytes accessed | tf_op | source)
XLA Modules:
  0.0 295.2 jit_solution(16655148561382840959)
XLA Ops:
  0.6 1.3 copy.12.pm_ref
  2.0 286.2 %shard_map.112 = (bf16[384,1536]{1,0:T(8,128)(2,1)}, bf16[384,1024]{1,0:T(8,128)(2,1)}, bf16[384,1024]{1,0:T(8,128)(2,1)}, bf16[1536,384]{1,0:T(8,128)(2,1)}, bf16[1536,384]{1,0:T(8,128)(2,1)}) custom-call(s32[16,1]{1,0:T(8,128)} %copy.12.pm_ref, bf16[384,1536]{1,0:T(8,128)(2,1)} %bitcast.17, bf16[384,1536]{1,0:T(8,128)(2,1)} %bitcast.18, ...), custom_call_target="tpu_custom_call" | custom-call | flops 6039797760 | bytes 25165824 | tf_op jit(solution)/shard_map/pallas_call | solution.py:486
  288.2 7.0 %shard_map.113 = (bf16[384,1536]{1,0:T(8,128)(2,1)}, bf16[1536,1024]{1,0:T(8,128)(2,1)}, bf16[1536,1024]{1,0:T(8,128)(2,1)}) custom-call(bf16[384,1536]{1,0:T(8,128)(2,1)} %get-tuple-element.11.state, bf16[384,1024]{1,0:T(8,128)(2,1)} %get-tuple-element.12.act, bf16[384,1024]{1,0:T(8,128)(2,1)} %get-tuple-element.13.pregrad, ...), custom_call_target="tpu_custom_call" | custom-call | flops 2415919104 | bytes 12582912 | tf_op jit(solution)/shard_map/pallas_call | solution.py:449
